TPU v7x, 32 devices: a whole 2x2x4 slice. The times are simulated.
32 devices in a mesh: groups: 2 (over x), wide: 16 (over z, y, core).
Axes of the slice: x: 2, y: 2, z: 4, core: 2. Of those that a mesh axis runs over, the one named last changes fastest.
Arguments:
- features: bfloat16 [4096, 512], P(('groups', 'wide')), parts along dimension 0, may hold values from -3.5 to 3.5
- centres: bfloat16 [8192, 512], P(('groups', 'wide')), parts along dimension 0, may hold values from -3.5 to 3.5
- targets: bfloat16 [4096, 128], P(('groups', 'wide')), parts along dimension 0, may hold values from -8 to 8
- coefficients: float32 [8192, 128], P(('groups', 'wide')), parts along dimension 0, may hold values from -1.6 to 1.6
- momentum: float32 [8192, 128], P(('groups', 'wide')), parts along dimension 0, may hold values from -0.8 to 0.8
- block_inverse: float32 [32, 256, 256], P(('groups', 'wide')), parts along dimension 0, may hold values from -3 to 3
Outputs:
- residual: float32 [4096, 128], P(('groups', 'wide')), parts along dimension 0
- new_momentum: float32 [8192, 128], P(('groups', 'wide')), parts along dimension 0
- new_coefficients: float32 [8192, 128], P(('groups', 'wide')), parts along dimension 0
There are 2 independent parts, one for each index of `groups`. A program takes and returns all parts, laid end to end along the dimension named above; each array names one. Nothing has to cross between parts.
All inputs are finite; a program needn't handle non-finite values.
Results may differ from a plain program's by a relative error of at most 0.0033.
Values may be sent and summed in bfloat16 or wider, within the bound.
A program may use at most 128 MiB of HBM per device.

v0:
```python
import jax
import jax.numpy as jnp
from jax import lax
from jax.sharding import PartitionSpec as P


def shards(features, centres, targets, coefficients, momentum, block_inverse):
    width = features.shape[1]
    centre_norms = jnp.sum(centres.astype(jnp.float32) ** 2, axis=1)
    shard_rows = lax.all_gather(features, "wide", axis=0, tiled=True)
    row_norms = jnp.sum(shard_rows.astype(jnp.float32) ** 2, axis=1)
    products = jnp.dot(shard_rows, centres.T, preferred_element_type=jnp.float32)
    kernel = jnp.exp(
        (2.0 * products - row_norms[:, None] - centre_norms[None, :]) * (2.0 / width)
    ).astype(jnp.bfloat16)
    batch_size = kernel.shape[0]
    coef_half = coefficients.astype(jnp.bfloat16)
    prediction = lax.psum_scatter(
        jnp.dot(kernel, coef_half, preferred_element_type=jnp.float32),
        "wide",
        scatter_dimension=0,
        tiled=True,
    )
    residual = prediction - targets.astype(jnp.float32)
    residual_half = lax.all_gather(residual.astype(jnp.bfloat16), "wide", axis=0, tiled=True)
    gradient = lax.dot_general(
        kernel, residual_half, (((0,), (0,)), ((), ())), preferred_element_type=jnp.float32
    )
    nblocks = block_inverse.shape[0]
    order = block_inverse.shape[1]
    grad_blocks = gradient.reshape(nblocks, order, gradient.shape[1])
    conditioned = jnp.einsum(
        "bij,bjk->bik", block_inverse, grad_blocks, precision=lax.Precision.HIGHEST
    )
    new_momentum = 0.9 * momentum + conditioned.reshape(gradient.shape) / batch_size
    new_coefficients = coefficients - 0.5 * new_momentum
    return (residual, new_momentum, new_coefficients)


def solution(mesh):
    in_specs = (
        P(("groups", "wide"), None),
        P(("groups", "wide"), None),
        P(("groups", "wide"), None),
        P(("groups", "wide"), None),
        P(("groups", "wide"), None),
        P(("groups", "wide"), None, None),
    )
    out_specs = (
        P(("groups", "wide"), None),
        P(("groups", "wide"), None),
        P(("groups", "wide"), None),
    )
    return jax.shard_map(shards, mesh=mesh, in_specs=in_specs, out_specs=out_specs, check_vma=False)
```

profile of v0, /device:TPU:1, one launch (start us, length us, event | category | flops | bytes accessed | tf_op | source)
XLA Modules:
  0.0 146.7 jit_solution(18435210653149370365)
XLA Ops:
  7.2 0.0 copy-start
  7.2 0.0 copy-start.3
  7.2 0.0 all-gather.2.cloned.1.call-start
  7.2 0.7 all-gather.2.cloned.1.call-update
  7.9 0.0 reduce-scatter.2.cloned.1.call-start
  8.0 1.1 multiply_reduce_fusion.1
  9.1 45.1 %all-gather.2.cloned.1.call-done = bf16[2048,512]{1,0:T(8,128)(2,1)} async-done(((bf16[128,512]{1,0:T(8,128)(2,1)}), bf16[2048,512]{1,0:T(8,128)(2,1)}) %all-gather.2.cloned.1.call-update) | async-done | bytes 2097168 | tf_op jit(solution)/shard_map/all_gather | solution.py:10
  54.1 0.0 copy-start.1
  54.1 2.2 %multiply_reduce_fusion = f32[2048]{0:T(1024)S(1)} fusion(bf16[2048,512]{1,0:T(8,128)(2,1)} %all-gather.2.cloned.1.call-done), kind=kLoop, calls=%fused_computation | loop fusion | flops 3143680 | bytes 2105344 | tf_op jit(solution)/shard_map/reduce_sum | solution.py:11
  56.3 0.0 copy-done.3
  56.4 0.0 copy-done.1
  56.4 0.0 copy-start.2
  56.4 0.7 fusion.4
  57.1 0.1 copy-done.2
  57.3 0.0 copy-start.4
  57.3 0.0 copy-start.5
  57.3 1.4 fusion.8
  58.7 0.0 reduce-scatter.2.cloned.1.call-update
  58.7 0.1 copy.10
  58.8 0.0 copy-done.4
  58.8 0.1 copy.9
  58.9 53.8 %reduce-scatter.2.cloned.1.call-done = f32[128,128]{1,0:T(8,128)} async-done(((f32[2048,128]{1,0:T(8,128)}), f32[128,128]{1,0:T(8,128)}) %reduce-scatter.2.cloned.1.call-update) | async-done | bytes 65552 | tf_op jit(solution)/shard_map/reduce_scatter | solution.py:18
  112.7 0.0 copy-done.5
  112.7 1.5 %fusion.10 = (bf16[128,128]{1,0:T(8,128)(2,1)S(1)}, f32[128,128]{1,0:T(8,128)}) fusion(f32[128,128]{1,0:T(8,128)} %reduce-scatter.2.cloned.1.call-done, bf16[128,128]{1,0:T(8,128)(2,1)S(1)} %copy-done.5), kind=kLoop, calls=%fused_computation.16 | loop fusion | flops 49152 | bytes 196608 | tf_op jit(solution)/shard_map/convert_element_type | solution.py:25
  114.2 23.2 %all_gather.7 = bf16[2048,128]{1,0:T(8,128)(2,1)S(1)} all-gather(bf16[128,128]{1,0:T(8,128)(2,1)S(1)} %get-tuple-element.6), channel_id=1, replica_groups=mesh['groups'=2,'wide'=16] {'wide'}, dimensions={0}, use_global_device_ids=true | all-gather | bytes 557056 | tf_op jit(solution)/shard_map/all_gather | solution.py:25
  137.4 0.5 fusion.11
  137.9 0.0 copy-done
  137.9 0.4 multiply_subtract_fusion
  138.3 0.8 copy.12
  139.1 0.8 copy.11
Async XLA Ops:
  7.2 130.8 %copy-start = (f32[1,256,256]{2,1,0:T(8,128)S(1)}, f32[1,256,256]{2,1,0:T(8,128)}, u32[]{:S(2)}) copy-start(f32[1,256,256]{2,1,0:T(8,128)} %param.11) | copy-start | bytes 786436
  7.2 49.2 %copy-start.3 = (bf16[256,512]{1,0:T(8,128)(2,1)S(1)}, bf16[256,512]{1,0:T(8,128)(2,1)}, u32[]{:S(2)}) copy-start(bf16[256,512]{1,0:T(8,128)(2,1)} %param.7) | copy-start | bytes 786436
  7.2 46.9 %all-gather.2.cloned.1.call-start = ((), (), s32[]{:S(2)}) async-start(), calls=%async_computation.1 | async-start | bytes 2228224 | tf_op jit(solution)/shard_map/all_gather | solution.py:10
  7.9 104.8 %reduce-scatter.2.cloned.1.call-start = ((), (), s32[]{:S(2)}) async-start(), calls=%async_computation.2 | async-start | bytes 1114112 | tf_op jit(solution)/shard_map/reduce_scatter | solution.py:18
  54.1 2.2 %copy-start.1 = (bf16[2048,512]{1,0:T(8,128)(2,1)S(1)}, bf16[2048,512]{1,0:T(8,128)(2,1)}, u32[]{:S(2)}) copy-start(bf16[2048,512]{1,0:T(8,128)(2,1)} %all-gather.2.cloned.1.call-done) | copy-start | bytes 6291460
  56.4 0.9 copy-start.2
  57.3 1.5 %copy-start.4 = (f32[256,128]{1,0:T(8,128)S(1)}, f32[256,128]{1,0:T(8,128)}, u32[]{:S(2)}) copy-start(f32[256,128]{1,0:T(8,128)} %param.10) | copy-start | bytes 393220
  57.3 55.5 %copy-start.5 = (bf16[128,128]{1,0:T(8,128)(2,1)S(1)}, bf16[128,128]{1,0:T(8,128)(2,1)}, u32[]{:S(2)}) copy-start(bf16[128,128]{1,0:T(8,128)(2,1)} %param.8) | copy-start | bytes 98308
Sparse Core Ops, SparseCore 0:
  10.2 43.8 all-gather.1
  58.8 53.8 reduce-scatter.1
where the time goes:
time: 147 us
  waiting for transfers between devices  99.6 us (68%)
  blocking collectives  23.2 us (16%)
  between operations  14.1 us (10%)
  other arithmetic  4.78 us (3%)
  matrix products  3.03 us (2%)
  local copies, waits for them, and re-layouts  1.87 us (1%)
    reduce_scatter x1, waiting for transfers between devices, shards(): lax.psum_scatter(jnp.dot(kernel, coef_half, preferred_element_type=jnp.fl...  53.8 us
    all_gather x1, waiting for transfers between devices, shards(): shard_rows = lax.all_gather(features, 'wide', axis=0, tiled=True)  45.1 us
    all_gather x1, blocking collectives, shards(): lax.all_gather(residual.astype(jnp.bfloat16), 'wide', axis=0, tiled=True)  23.2 us
  transfers between devices with their start and end apart: 2, of which 2 were waited for; matrix products, arithmetic and copies ran while one was open for 1% of the time, Pallas kernels for 0%

commit v1 on v0

v1 whole, which is shorter than its diff:
```python
import functools

import jax
import jax.numpy as jnp
from jax import lax
from jax.experimental import pallas as pl
from jax.experimental.pallas import tpu as pltpu
from jax.sharding import PartitionSpec as P

MESH = pl.DeviceIdType.MESH
PRED = jnp.float32
GRAD = jnp.float32


def kernel(
    A, B, batch,
    feat, cen, targ, coef, mom, inv,
    res_out, mom_out, coef_out,
    rows, rnorm, cens, cnorm, coefs, kt, own_pred, pred_tx, pred_rx, resid, g_own, g_tx, g_rx,
    row_ss, row_rs, cen_ss, cen_rs, cf_ss, cf_rs, pr_ss, pr_rs, re_ss, re_rs, g_ss, g_rs,
):
    w = lax.axis_index("wide")
    c = lax.rem(w, 2)
    chip = w // 2
    b = lax.rem(chip, B)
    a = chip // B
    R = feat.shape[0]
    scale = 2.0 / feat.shape[1]

    def dev(aa, bb, cc):
        return {"wide": (aa * B + bb) * 2 + cc}

    def put(src, dst, ss, rs, to):
        return pltpu.make_async_remote_copy(
            src_ref=src, dst_ref=dst, send_sem=ss, recv_sem=rs, device_id=to, device_id_type=MESH
        )

    me_cb = b * 2 + c
    mate_cb = b * 2 + (1 - c)
    mate = dev(a, b, 1 - c)

    barrier = pltpu.get_barrier_semaphore()
    for j in range(1, A):
        pl.semaphore_signal(barrier, inc=1, device_id=dev(lax.rem(a + j, A), b, c), device_id_type=MESH)
    for j in range(B):
        for k in range(2):
            if j or k:
                pl.semaphore_signal(
                    barrier, inc=1, device_id=dev(a, lax.rem(b + j, B), lax.rem(c + k, 2)), device_id_type=MESH
                )

    rows[a] = feat[...]
    cens[me_cb] = cen[...]
    coefs[me_cb] = coef[...].astype(jnp.bfloat16).T

    def row_copy(block, d):
        to = a + 1 if d == 0 else a - 1
        return put(rows.at[block], rows.at[block], row_ss.at[block, d], row_rs.at[block], dev(to, b, c))

    def cen_copy(cb, slot, to):
        return put(cens.at[cb], cens.at[cb], cen_ss.at[slot], cen_rs.at[cb], to)

    def coef_copy(cb, slot, to):
        return put(coefs.at[cb], coefs.at[cb], cf_ss.at[slot], cf_rs.at[cb], to)

    pl.semaphore_wait(barrier, A - 1 + 2 * B - 1)

    @pl.when(a < A - 1)
    def _():
        row_copy(a, 0).start()

    @pl.when(a > 0)
    def _():
        row_copy(a, 1).start()

    for j in range(1, B):
        bb = lax.rem(b + j, B)
        cen_copy(me_cb, bb, dev(a, bb, c)).start()
        coef_copy(me_cb, bb, dev(a, bb, c)).start()
    cen_copy(me_cb, B + b, mate).start()
    coef_copy(me_cb, B + b, mate).start()

    def row_norm(block):
        x = rows[block].astype(jnp.float32)
        s = jnp.sum(x * x, axis=1, keepdims=True)
        rnorm[block] = jnp.broadcast_to(s, (R, 128)).T[0:8]

    def cen_norm(cb):
        x = cens[cb].astype(jnp.float32)
        s = jnp.sum(x * x, axis=1, keepdims=True)
        cnorm[cb] = jnp.broadcast_to(s, (x.shape[0], 128))

    def tile(block, cb):
        p = lax.dot_general(
            cens[cb], rows[block], (((1,), (1,)), ((), ())), preferred_element_type=jnp.float32
        )
        e = (2.0 * p - rnorm[block, 0:1, :] - cnorm[cb, :, 0:1]) * scale
        kt[cb, :, pl.ds(pl.multiple_of(block * R, R), R)] = jnp.exp(e).astype(jnp.bfloat16)

    def tiles(block, lo, hi):
        def step(i, carry):
            tile(block, lax.rem(b + i // 2, B) * 2 + lax.rem(c + lax.rem(i, 2), 2))
            return carry

        lax.fori_loop(lo, hi, step, 0, unroll=2)

    def predict(block):
        def step(i, acc):
            k = kt[i, :, pl.ds(pl.multiple_of(block * R, R), R)]
            return acc + jnp.dot(coefs[i], k, preferred_element_type=jnp.float32)

        return lax.fori_loop(0, 2 * B, step, jnp.zeros((coefs.shape[1], R), jnp.float32), unroll=2)

    def pred_copy(block):
        return put(pred_tx.at[block], pred_rx.at[a], pr_ss.at[block], pr_rs.at[a], dev(block, b, c))

    def predict_and_send(block):
        pred_tx[block] = predict(block).astype(PRED)
        pred_copy(block).start()

    def each_at(dist, fn):
        @pl.when(a - dist >= 0)
        def _():
            fn(a - dist, 0)

        @pl.when(a + dist < A)
        def _():
            fn(a + dist, 1)

    def take_rows(block, d):
        row_copy(block, d).wait_recv()
        if d == 0:
            @pl.when(a < A - 1)
            def _():
                row_copy(block, 0).start()
        else:
            @pl.when(a > 0)
            def _():
                row_copy(block, 1).start()
        row_norm(block)
        tiles(block, 0, 2)

    row_norm(a)
    cen_norm(me_cb)
    tile(a, me_cb)
    cen_copy(mate_cb, 0, mate).wait_recv()
    coef_copy(mate_cb, 0, mate).wait_recv()
    cen_norm(mate_cb)
    tile(a, mate_cb)

    each_at(1, take_rows)

    for j in range(1, B):
        bb = lax.rem(b + j, B)
        cen_copy(bb * 2 + c, 0, mate).wait_recv()
        cen_copy(bb * 2 + c, B + bb, mate).start()
        coef_copy(bb * 2 + c, 0, mate).wait_recv()
        coef_copy(bb * 2 + c, B + bb, mate).start()
        cen_norm(bb * 2 + c)

    for dist in range(2, A - 1):
        each_at(dist, take_rows)

    for j in range(1, B):
        bb = lax.rem(b + j, B)
        cen_copy(bb * 2 + 1 - c, 0, mate).wait_recv()
        coef_copy(bb * 2 + 1 - c, 0, mate).wait_recv()
        cen_norm(bb * 2 + 1 - c)

    def finish(block, d):
        tiles(block, 2, 2 * B)
        predict_and_send(block)

    for dist in range(1, A - 1):
        each_at(dist, finish)
    tiles(a, 2, 2 * B)
    own_pred[...] = predict(a)

    def last(block, d):
        take_rows(block, d)
        finish(block, d)

    each_at(A - 1, last)

    total = own_pred[...]
    for j in range(1, A):
        aa = lax.rem(a + j, A)
        put(pred_tx.at[aa], pred_rx.at[aa], pr_ss.at[aa], pr_rs.at[aa], dev(aa, b, c)).wait_recv()
        total = total + pred_rx[aa].astype(jnp.float32)
    res = total.T - targ[...].astype(jnp.float32)
    resid[a] = res.astype(jnp.bfloat16)

    def res_copy(block, to):
        return put(resid.at[block], resid.at[block], re_ss.at[to], re_rs.at[block], dev(to, b, c))

    for j in range(1, A):
        res_copy(a, lax.rem(a + j, A)).start()
    res_out[...] = res
    for j in range(1, A):
        aa = lax.rem(a + j, A)
        res_copy(aa, aa).wait_recv()

    r = resid[...].reshape(A * R, resid.shape[2])

    def g_copy(cb, bb, cc):
        return put(g_tx.at[cb], g_rx.at[me_cb], g_ss.at[cb], g_rs.at[me_cb], dev(a, bb, cc))

    order = [(j, k) for j in range(1, B) for k in range(2)] + [(0, 1)]
    for j, k in order:
        bb, cc = lax.rem(b + j, B), lax.rem(c + k, 2)
        cb = bb * 2 + cc
        g_tx[cb] = jnp.dot(kt[cb], r, preferred_element_type=jnp.float32).astype(GRAD)
        g_copy(cb, bb, cc).start()
    g = jnp.dot(kt[me_cb], r, preferred_element_type=jnp.float32)
    for j, k in reversed(order):
        bb, cc = lax.rem(b + j, B), lax.rem(c + k, 2)
        cb = bb * 2 + cc
        put(g_tx.at[cb], g_rx.at[cb], g_ss.at[cb], g_rs.at[cb], dev(a, bb, cc)).wait_recv()
        g = g + g_rx[cb].astype(jnp.float32)
    g_own[...] = g

    n = inv.shape[1]
    for i in range(inv.shape[0]):
        at = pl.ds(i * n, n)
        cond = jnp.dot(
            inv[i], g_own[at, :], precision=lax.Precision.HIGHEST, preferred_element_type=jnp.float32
        )
        new = 0.9 * mom[at, :] + cond / batch
        mom_out[at, :] = new
        coef_out[at, :] = coef[at, :] - 0.5 * new

    @pl.when(a < A - 1)
    def _():
        row_copy(a, 0).wait_send()

    @pl.when(a > 0)
    def _():
        row_copy(a, 1).wait_send()

    def sent_rows(block, d):
        if d == 0:
            @pl.when(a < A - 1)
            def _():
                row_copy(block, 0).wait_send()
        else:
            @pl.when(a > 0)
            def _():
                row_copy(block, 1).wait_send()

    for dist in range(1, A):
        each_at(dist, sent_rows)
    for j in range(1, B):
        bb = lax.rem(b + j, B)
        for slot in (bb, B + bb):
            cen_copy(me_cb, slot, mate).wait_send()
            coef_copy(me_cb, slot, mate).wait_send()
    cen_copy(me_cb, B + b, mate).wait_send()
    coef_copy(me_cb, B + b, mate).wait_send()
    for j in range(1, A):
        aa = lax.rem(a + j, A)
        pred_copy(aa).wait_send()
        res_copy(a, aa).wait_send()
    for j, k in order:
        bb, cc = lax.rem(b + j, B), lax.rem(c + k, 2)
        g_copy(bb * 2 + cc, bb, cc).wait_send()


def shards(A, B, features, centres, targets, coefficients, momentum, block_inverse):
    R, D = features.shape
    C, K = coefficients.shape
    G = 2 * B
    dma = pltpu.SemaphoreType.DMA
    vmem = pl.BlockSpec(memory_space=pltpu.VMEM)
    flops = 2 * A * R * G * C * (D + 2 * K)
    return pl.pallas_call(
        functools.partial(kernel, A, B, float(A * B * 2 * R)),
        out_shape=(
            jax.ShapeDtypeStruct((R, K), jnp.float32),
            jax.ShapeDtypeStruct((C, K), jnp.float32),
            jax.ShapeDtypeStruct((C, K), jnp.float32),
        ),
        in_specs=[vmem] * 6,
        out_specs=(vmem,) * 3,
        scratch_shapes=[
            pltpu.VMEM((A, R, D), jnp.bfloat16),
            pltpu.VMEM((A, 8, R), jnp.float32),
            pltpu.VMEM((G, C, D), jnp.bfloat16),
            pltpu.VMEM((G, C, 128), jnp.float32),
            pltpu.VMEM((G, K, C), jnp.bfloat16),
            pltpu.VMEM((G, C, A * R), jnp.bfloat16),
            pltpu.VMEM((K, R), jnp.float32),
            pltpu.VMEM((A, K, R), PRED),
            pltpu.VMEM((A, K, R), PRED),
            pltpu.VMEM((A, R, K), jnp.bfloat16),
            pltpu.VMEM((C, K), jnp.float32),
            pltpu.VMEM((G, C, K), GRAD),
            pltpu.VMEM((G, C, K), GRAD),
            dma((A, 2)), dma((A,)),
            dma((G,)), dma((G,)), dma((G,)), dma((G,)),
            dma((A,)), dma((A,)), dma((A,)), dma((A,)),
            dma((G,)), dma((G,)),
        ],
        compiler_params=pltpu.CompilerParams(
            collective_id=0, has_side_effects=True, vmem_limit_bytes=40 * 1024 * 1024
        ),
        cost_estimate=pl.CostEstimate(
            flops=flops, bytes_accessed=4 * C * (C + 4 * K), transcendentals=A * R * G * C
        ),
    )(features, centres, targets, coefficients, momentum, block_inverse)


def solution(mesh):
    chips = mesh.shape["wide"] // 2
    B = 1 << ((chips.bit_length() - 1) // 2)
    A = chips // B
    two = P(("groups", "wide"), None)
    return jax.shard_map(
        functools.partial(shards, A, B),
        mesh=mesh,
        in_specs=(two, two, two, two, two, P(("groups", "wide"), None, None)),
        out_specs=(two, two, two),
        check_vma=False,
    )
```

time: 147 us -> 42.4 us (0.29)
  waiting for transfers between devices: 99.6 us -> 0 us
  Pallas kernels: 0 us -> 34 us
  blocking collectives: 23.2 us -> 0 us
  between operations: 14.1 us -> 0.65 us
  local copies, waits for them, and re-layouts: 1.87 us -> 7.3 us
  other arithmetic: 4.78 us -> 0 us
  matrix products: 3.03 us -> 0 us
    reduce_scatter x1 -> x0, waiting for transfers between devices: 53.8 us -> none  [shards(): lax.psum_scatter(jnp.dot(kernel, coef_half, preferred_element_type=jnp.fl...]
    all_gather x1 -> x0, waiting for transfers between devices: 45.1 us -> none  [shards(): shard_rows = lax.all_gather(features, 'wide', axis=0, tiled=True)]
    pallas_call x0 -> x1, Pallas kernels: none -> 34 us  [shards(): pl.pallas_call(functools.partial(kernel, A, B, float(A * B * 2 * R)), out...]
    all_gather x1 -> x0, blocking collectives: 23.2 us -> none  [shards(): lax.all_gather(residual.astype(jnp.bfloat16), 'wide', axis=0, tiled=True)]
    unnamed x16 -> x15, local copies, waits for them, and re-layouts: 1.87 us -> 7.3 us
    reduce_sum x2 -> x0, other arithmetic: 3.3 us -> none  [the longest x1 2.22 us: shards(): row_norms = jnp.sum(shard_rows.astype(jnp.float32) ** 2, axis=1)]
    dot_general x4 -> x0, matrix products: 3.03 us -> none  [the longest x1 1.41 us: shards(): jnp.dot(kernel, coef_half, preferred_element_type=jnp.float32)]
    convert_element_type x1 -> x0, other arithmetic: 1.48 us -> none  [shards(): residual.astype(jnp.bfloat16)]
  transfers between devices with their start and end apart: 2 -> 0, of which waited for: 2 -> 0; matrix products, arithmetic and copies ran while one was open for 1% -> 0% of each run, Pallas kernels for 0% -> 0%
where the time goes in v1:
time: 42.4 us; the launch traced here: 42 us
  Pallas kernels  34 us (80%)
  local copies, waits for them, and re-layouts  7.3 us (17%)
  between operations  0.65 us (2%)
    pallas_call x1, Pallas kernels, shards(): pl.pallas_call(functools.partial(kernel, A, B, float(A * B * 2 * R)), out...  34 us
    unnamed x15, local copies, waits for them, and re-layouts  7.3 us

profile of v1, /device:TPU:1, one launch (start us, length us, event | category | flops | bytes accessed | tf_op | source)
XLA Modules:
  0.0 42.0 jit_solution(18357089196851404513)
XLA Ops:
  0.6 0.0 copy-start
  0.6 0.9 %copy-done = bf16[256,512]{1,0:T(8,128)(2,1)S(1)} copy-done((bf16[256,512]{1,0:T(8,128)(2,1)S(1)}, bf16[256,512]{1,0:T(8,128)(2,1)}, u32[]{:S(2)}) %copy-start) | copy-done | bytes 262168
  1.6 0.0 copy-start.1
  1.6 0.9 %copy-done.1 = f32[1,256,256]{2,1,0:T(8,128)S(1)} copy-done((f32[1,256,256]{2,1,0:T(8,128)S(1)}, f32[1,256,256]{2,1,0:T(8,128)}, u32[]{:S(2)}) %copy-start.1) | copy-done | bytes 262168
  2.5 0.0 copy-start.2
  2.5 0.9 %copy-done.2 = bf16[128,512]{1,0:T(8,128)(2,1)S(1)} copy-done((bf16[128,512]{1,0:T(8,128)(2,1)S(1)}, bf16[128,512]{1,0:T(8,128)(2,1)}, u32[]{:S(2)}) %copy-start.2) | copy-done | bytes 131096
  3.4 0.0 copy-start.3
  3.4 0.9 %copy-done.3 = f32[256,128]{1,0:T(8,128)S(1)} copy-done((f32[256,128]{1,0:T(8,128)S(1)}, f32[256,128]{1,0:T(8,128)}, u32[]{:S(2)}) %copy-start.3) | copy-done | bytes 131096
  4.3 0.0 copy-start.4
  4.3 0.9 %copy-done.4 = f32[256,128]{1,0:T(8,128)S(1)} copy-done((f32[256,128]{1,0:T(8,128)S(1)}, f32[256,128]{1,0:T(8,128)}, u32[]{:S(2)}) %copy-start.4) | copy-done | bytes 131096
  5.2 0.0 copy-start.5
  5.2 0.8 %copy-done.5 = bf16[128,128]{1,0:T(8,128)(2,1)S(1)} copy-done((bf16[128,128]{1,0:T(8,128)(2,1)S(1)}, bf16[128,128]{1,0:T(8,128)(2,1)}, u32[]{:S(2)}) %copy-start.5) | copy-done | bytes 32792
  6.0 34.0 %shard_map.85 = (f32[128,128]{1,0:T(8,128)S(1)}, f32[256,128]{1,0:T(8,128)S(1)}, f32[256,128]{1,0:T(8,128)S(1)}) custom-call(bf16[128,512]{1,0:T(8,128)(2,1)S(1)} %copy-done.2, bf16[256,512]{1,0:T(8,128)(2,1)S(1)} %copy-done, bf16[128,128]{1,0:T(8,128)(2,1)S(1)} %copy-done.5, f32[256,128]{1,0:T(8,128)S(1)} %copy-done.3, f32[256,128]{1,0:T(8,128)S(1)} %copy-done.4, ...), custom_call_target="tpu_custom_call" | custom-call | flops 805306368 | bytes 786432 | tf_op jit(solution)/shard_map/pallas_call | solution.py:275
  40.0 0.6 %copy.12 = f32[128,128]{1,0:T(8,128)} copy(f32[128,128]{1,0:T(8,128)S(1)} %get-tuple-element.6) | data formatting | bytes 131072
  40.7 0.7 %copy.13 = f32[256,128]{1,0:T(8,128)} copy(f32[256,128]{1,0:T(8,128)S(1)} %get-tuple-element.7) | data formatting | bytes 262144
  41.3 0.7 %copy.14 = f32[256,128]{1,0:T(8,128)} copy(f32[256,128]{1,0:T(8,128)S(1)} %get-tuple-element.8) | data formatting | bytes 262144
Async XLA Ops:
  0.6 1.0 %copy-start = (bf16[256,512]{1,0:T(8,128)(2,1)S(1)}, bf16[256,512]{1,0:T(8,128)(2,1)}, u32[]{:S(2)}) copy-start(bf16[256,512]{1,0:T(8,128)(2,1)} %cen.1) | copy-start | bytes 786436
  1.6 0.9 %copy-start.1 = (f32[1,256,256]{2,1,0:T(8,128)S(1)}, f32[1,256,256]{2,1,0:T(8,128)}, u32[]{:S(2)}) copy-start(f32[1,256,256]{2,1,0:T(8,128)} %inv.1) | copy-start | bytes 786436
  2.5 0.9 %copy-start.2 = (bf16[128,512]{1,0:T(8,128)(2,1)S(1)}, bf16[128,512]{1,0:T(8,128)(2,1)}, u32[]{:S(2)}) copy-start(bf16[128,512]{1,0:T(8,128)(2,1)} %feat.1) | copy-start | bytes 393220
  3.4 0.9 %copy-start.3 = (f32[256,128]{1,0:T(8,128)S(1)}, f32[256,128]{1,0:T(8,128)}, u32[]{:S(2)}) copy-start(f32[256,128]{1,0:T(8,128)} %coef.1) | copy-start | bytes 393220
  4.3 0.9 %copy-start.4 = (f32[256,128]{1,0:T(8,128)S(1)}, f32[256,128]{1,0:T(8,128)}, u32[]{:S(2)}) copy-start(f32[256,128]{1,0:T(8,128)} %mom.1) | copy-start | bytes 393220
  5.2 0.8 %copy-start.5 = (bf16[128,128]{1,0:T(8,128)(2,1)S(1)}, bf16[128,128]{1,0:T(8,128)(2,1)}, u32[]{:S(2)}) copy-start(bf16[128,128]{1,0:T(8,128)(2,1)} %targ.1) | copy-start | bytes 98308

commit v2 on v1

--- a/solution.py
+++ b/solution.py
@@ -1,4 +1,5 @@
 import functools
+import itertools
 
 import jax
 import jax.numpy as jnp
@@ -8,14 +9,17 @@
 from jax.sharding import PartitionSpec as P
 
 MESH = pl.DeviceIdType.MESH
-PRED = jnp.float32
-GRAD = jnp.float32
+PRED = jnp.bfloat16
+GRAD = jnp.bfloat16
+H = 2
+Q = 4
 
 
 def kernel(
-    A, B, batch,
-    feat, cen, targ, coef, mom, inv,
-    res_out, mom_out, coef_out,
+    A, B,
+    feat, cen, targ, coef, inv,
+    res_out, cond_out,
+    coef_own, targ_own, inv_own, in_sem,
     rows, rnorm, cens, cnorm, coefs, kt, own_pred, pred_tx, pred_rx, resid, g_own, g_tx, g_rx,
     row_ss, row_rs, cen_ss, cen_rs, cf_ss, cf_rs, pr_ss, pr_rs, re_ss, re_rs, g_ss, g_rs,
 ):
@@ -24,7 +28,7 @@
     chip = w // 2
     b = lax.rem(chip, B)
     a = chip // B
-    R = feat.shape[0]
+    R, C = feat.shape[0], cen.shape[0]
     scale = 2.0 / feat.shape[1]
 
     def dev(aa, bb, cc):
@@ -49,35 +53,52 @@
                     barrier, inc=1, device_id=dev(a, lax.rem(b + j, B), lax.rem(c + k, 2)), device_id_type=MESH
                 )
 
-    rows[a] = feat[...]
-    cens[me_cb] = cen[...]
-    coefs[me_cb] = coef[...].astype(jnp.bfloat16).T
-
-    def row_copy(block, d):
+    loads = [
+        pltpu.make_async_copy(src, dst, in_sem.at[i])
+        for i, (src, dst) in enumerate(
+            [(feat, rows.at[a]), (cen, cens.at[me_cb]), (coef, coef_own), (targ, targ_own), (inv, inv_own)]
+        )
+    ]
+    for load in loads:
+        load.start()
+
+    def row_copy(block, d, h):
         to = a + 1 if d == 0 else a - 1
-        return put(rows.at[block], rows.at[block], row_ss.at[block, d], row_rs.at[block], dev(to, b, c))
-
-    def cen_copy(cb, slot, to):
-        return put(cens.at[cb], cens.at[cb], cen_ss.at[slot], cen_rs.at[cb], to)
+        part = rows.at[block, pl.ds(h * (R // H), R // H)]
+        return put(part, part, row_ss.at[block, d, h], row_rs.at[block, h], dev(to, b, c))
+
+    def cen_copy(cb, slot, q, to):
+        part = cens.at[cb, pl.ds(q * (C // Q), C // Q)]
+        return put(part, part, cen_ss.at[slot, q], cen_rs.at[cb, q], to)
 
     def coef_copy(cb, slot, to):
         return put(coefs.at[cb], coefs.at[cb], cf_ss.at[slot], cf_rs.at[cb], to)
 
+    loads[0].wait()
+    loads[1].wait()
     pl.semaphore_wait(barrier, A - 1 + 2 * B - 1)
 
     @pl.when(a < A - 1)
     def _():
-        row_copy(a, 0).start()
+        for h in range(H):
+            row_copy(a, 0, h).start()
 
     @pl.when(a > 0)
     def _():
-        row_copy(a, 1).start()
-
-    for j in range(1, B):
-        bb = lax.rem(b + j, B)
-        cen_copy(me_cb, bb, dev(a, bb, c)).start()
+        for h in range(H):
+            row_copy(a, 1, h).start()
+
+    for j in range(1, B):
+        bb = lax.rem(b + j, B)
+        for q in range(Q):
+            cen_copy(me_cb, bb, q, dev(a, bb, c)).start()
+    for q in range(Q):
+        cen_copy(me_cb, B + b, q, mate).start()
+    loads[2].wait()
+    coefs[me_cb] = coef_own[...].astype(jnp.bfloat16).T
+    for j in range(1, B):
+        bb = lax.rem(b + j, B)
         coef_copy(me_cb, bb, dev(a, bb, c)).start()
-    cen_copy(me_cb, B + b, mate).start()
     coef_copy(me_cb, B + b, mate).start()
 
     def row_norm(block):
@@ -127,67 +148,85 @@
         def _():
             fn(a + dist, 1)
 
-    def take_rows(block, d):
-        row_copy(block, d).wait_recv()
+    def pass_rows(h, block, d):
+        row_copy(block, d, h).wait_recv()
         if d == 0:
             @pl.when(a < A - 1)
             def _():
-                row_copy(block, 0).start()
+                row_copy(block, 0, h).start()
         else:
             @pl.when(a > 0)
             def _():
-                row_copy(block, 1).start()
+                row_copy(block, 1, h).start()
+
+    def near(block, d):
         row_norm(block)
         tiles(block, 0, 2)
+
+    def pass_centres(j, q):
+        bb = lax.rem(b + j, B)
+        cen_copy(bb * 2 + c, 0, q, mate).wait_recv()
+        cen_copy(bb * 2 + c, B + bb, q, mate).start()
 
     row_norm(a)
     cen_norm(me_cb)
     tile(a, me_cb)
-    cen_copy(mate_cb, 0, mate).wait_recv()
-    coef_copy(mate_cb, 0, mate).wait_recv()
+    for q in range(Q):
+        cen_copy(mate_cb, 0, q, mate).wait_recv()
     cen_norm(mate_cb)
     tile(a, mate_cb)
 
-    each_at(1, take_rows)
-
-    for j in range(1, B):
-        bb = lax.rem(b + j, B)
-        cen_copy(bb * 2 + c, 0, mate).wait_recv()
-        cen_copy(bb * 2 + c, B + bb, mate).start()
+    steps = itertools.zip_longest(
+        [(dist, h) for dist in range(1, A - 1) for h in range(H)],
+        [(j, q) for j in range(1, B) for q in range(Q)],
+    )
+    for row_step, cen_step in steps:
+        if row_step is not None:
+            dist, h = row_step
+            each_at(dist, functools.partial(pass_rows, h))
+        if cen_step is not None:
+            pass_centres(*cen_step)
+        if row_step is not None and h == H - 1:
+            each_at(dist, near)
+
+    for j in range(1, B):
+        bb = lax.rem(b + j, B)
         coef_copy(bb * 2 + c, 0, mate).wait_recv()
         coef_copy(bb * 2 + c, B + bb, mate).start()
         cen_norm(bb * 2 + c)
-
-    for dist in range(2, A - 1):
-        each_at(dist, take_rows)
-
-    for j in range(1, B):
-        bb = lax.rem(b + j, B)
-        cen_copy(bb * 2 + 1 - c, 0, mate).wait_recv()
-        coef_copy(bb * 2 + 1 - c, 0, mate).wait_recv()
+    for j in range(1, B):
+        bb = lax.rem(b + j, B)
+        for q in range(Q):
+            cen_copy(bb * 2 + 1 - c, 0, q, mate).wait_recv()
         cen_norm(bb * 2 + 1 - c)
-
-    def finish(block, d):
-        tiles(block, 2, 2 * B)
+    for dist in range(1, A - 1):
+        each_at(dist, lambda block, d: tiles(block, 2, 2 * B))
+    tiles(a, 2, 2 * B)
+
+    coef_copy(mate_cb, 0, mate).wait_recv()
+    for j in range(1, B):
+        coef_copy(lax.rem(b + j, B) * 2 + 1 - c, 0, mate).wait_recv()
+    for dist in range(A - 2, 0, -1):
+        each_at(dist, lambda block, d: predict_and_send(block))
+
+    def last(block, d):
+        for h in range(H):
+            pass_rows(h, block, d)
+        row_norm(block)
+        tiles(block, 0, 2 * B)
         predict_and_send(block)
 
-    for dist in range(1, A - 1):
-        each_at(dist, finish)
-    tiles(a, 2, 2 * B)
+    each_at(A - 1, last)
     own_pred[...] = predict(a)
-
-    def last(block, d):
-        take_rows(block, d)
-        finish(block, d)
-
-    each_at(A - 1, last)
+    loads[3].wait()
+    loads[4].wait()
 
     total = own_pred[...]
     for j in range(1, A):
         aa = lax.rem(a + j, A)
         put(pred_tx.at[aa], pred_rx.at[aa], pr_ss.at[aa], pr_rs.at[aa], dev(aa, b, c)).wait_recv()
         total = total + pred_rx[aa].astype(jnp.float32)
-    res = total.T - targ[...].astype(jnp.float32)
+    res = total.T - targ_own[...].astype(jnp.float32)
     resid[a] = res.astype(jnp.bfloat16)
 
     def res_copy(block, to):
@@ -222,39 +261,34 @@
     n = inv.shape[1]
     for i in range(inv.shape[0]):
         at = pl.ds(i * n, n)
-        cond = jnp.dot(
-            inv[i], g_own[at, :], precision=lax.Precision.HIGHEST, preferred_element_type=jnp.float32
+        cond_out[at, :] = jnp.dot(
+            inv_own[i], g_own[at, :], precision=lax.Precision.HIGHEST, preferred_element_type=jnp.float32
         )
-        new = 0.9 * mom[at, :] + cond / batch
-        mom_out[at, :] = new
-        coef_out[at, :] = coef[at, :] - 0.5 * new
-
-    @pl.when(a < A - 1)
-    def _():
-        row_copy(a, 0).wait_send()
-
-    @pl.when(a > 0)
-    def _():
-        row_copy(a, 1).wait_send()
 
     def sent_rows(block, d):
         if d == 0:
             @pl.when(a < A - 1)
             def _():
-                row_copy(block, 0).wait_send()
+                for h in range(H):
+                    row_copy(block, 0, h).wait_send()
         else:
             @pl.when(a > 0)
             def _():
-                row_copy(block, 1).wait_send()
-
+                for h in range(H):
+                    row_copy(block, 1, h).wait_send()
+
+    sent_rows(a, 0)
+    sent_rows(a, 1)
     for dist in range(1, A):
         each_at(dist, sent_rows)
     for j in range(1, B):
         bb = lax.rem(b + j, B)
         for slot in (bb, B + bb):
-            cen_copy(me_cb, slot, mate).wait_send()
+            for q in range(Q):
+                cen_copy(me_cb, slot, q, mate).wait_send()
             coef_copy(me_cb, slot, mate).wait_send()
-    cen_copy(me_cb, B + b, mate).wait_send()
+    for q in range(Q):
+        cen_copy(me_cb, B + b, q, mate).wait_send()
     coef_copy(me_cb, B + b, mate).wait_send()
     for j in range(1, A):
         aa = lax.rem(a + j, A)
@@ -271,17 +305,17 @@
     G = 2 * B
     dma = pltpu.SemaphoreType.DMA
     vmem = pl.BlockSpec(memory_space=pltpu.VMEM)
-    flops = 2 * A * R * G * C * (D + 2 * K)
-    return pl.pallas_call(
-        functools.partial(kernel, A, B, float(A * B * 2 * R)),
-        out_shape=(
-            jax.ShapeDtypeStruct((R, K), jnp.float32),
-            jax.ShapeDtypeStruct((C, K), jnp.float32),
-            jax.ShapeDtypeStruct((C, K), jnp.float32),
-        ),
-        in_specs=[vmem] * 6,
-        out_specs=(vmem,) * 3,
+    hbm = pl.BlockSpec(memory_space=pltpu.HBM)
+    residual, conditioned = pl.pallas_call(
+        functools.partial(kernel, A, B),
+        out_shape=(jax.ShapeDtypeStruct((R, K), jnp.float32), jax.ShapeDtypeStruct((C, K), jnp.float32)),
+        in_specs=[hbm] * 5,
+        out_specs=(vmem,) * 2,
         scratch_shapes=[
+            pltpu.VMEM((C, K), jnp.float32),
+            pltpu.VMEM((R, K), jnp.bfloat16),
+            pltpu.VMEM(block_inverse.shape, jnp.float32),
+            dma((5,)),
             pltpu.VMEM((A, R, D), jnp.bfloat16),
             pltpu.VMEM((A, 8, R), jnp.float32),
             pltpu.VMEM((G, C, D), jnp.bfloat16),
@@ -295,18 +329,22 @@
             pltpu.VMEM((C, K), jnp.float32),
             pltpu.VMEM((G, C, K), GRAD),
             pltpu.VMEM((G, C, K), GRAD),
-            dma((A, 2)), dma((A,)),
-            dma((G,)), dma((G,)), dma((G,)), dma((G,)),
+            dma((A, 2, H)), dma((A, H)),
+            dma((G, Q)), dma((G, Q)), dma((G,)), dma((G,)),
             dma((A,)), dma((A,)), dma((A,)), dma((A,)),
             dma((G,)), dma((G,)),
         ],
         compiler_params=pltpu.CompilerParams(
-            collective_id=0, has_side_effects=True, vmem_limit_bytes=40 * 1024 * 1024
+            collective_id=0, has_side_effects=True, vmem_limit_bytes=63 * 1024 * 1024
         ),
         cost_estimate=pl.CostEstimate(
-            flops=flops, bytes_accessed=4 * C * (C + 4 * K), transcendentals=A * R * G * C
+            flops=2 * A * R * G * C * (D + 2 * K),
+            bytes_accessed=4 * C * (C + 4 * K),
+            transcendentals=A * R * G * C,
         ),
-    )(features, centres, targets, coefficients, momentum, block_inverse)
+    )(features, centres, targets, coefficients, block_inverse)
+    new_momentum = 0.9 * momentum + conditioned / (A * B * 2 * R)
+    return residual, new_momentum, coefficients - 0.5 * new_momentum
 
 
 def solution(mesh):

time: 42.4 us -> 34.9 us (0.82)
  local copies, waits for them, and re-layouts: 7.3 us -> 0.64 us
  Pallas kernels: 34 us -> 31.7 us
  other arithmetic: 0 us -> 1.66 us
    unnamed x15 -> x7, local copies, waits for them, and re-layouts: 7.3 us -> 0.64 us
    pallas_call x1, Pallas kernels: 34 us -> 31.7 us  [shards(): pl.pallas_call(functools.partial(kernel, A, B), out_shape=(jax.ShapeDtype...]
    sub x0 -> x1, other arithmetic: none -> 1.66 us  [shards(): return (residual, new_momentum, coefficients - 0.5 * new_momentum)]
where the time goes in v2:
time: 34.9 us; the launch traced here: 34.7 us
  Pallas kernels  31.7 us (91%)
  other arithmetic  1.66 us (5%)
  between operations  0.68 us (2%)
  local copies, waits for them, and re-layouts  0.64 us (2%)
    pallas_call x1, Pallas kernels, shards(): pl.pallas_call(functools.partial(kernel, A, B), out_shape=(jax.ShapeDtype...  31.7 us
    sub x1, other arithmetic, shards(): return (residual, new_momentum, coefficients - 0.5 * new_momentum)  1.66 us

profile of v2, /device:TPU:1, one launch (start us, length us, event | category | flops | bytes accessed | tf_op | source)
XLA Modules:
  0.0 34.7 jit_solution(16176442766969616251)
XLA Ops:
  0.6 0.0 copy-start
  0.6 0.0 copy-start.1
  0.7 31.7 %shard_map.85 = (f32[128,128]{1,0:T(8,128)}, f32[256,128]{1,0:T(8,128)}) custom-call(bf16[128,512]{1,0:T(8,128)(2,1)} %feat.1, bf16[256,512]{1,0:T(8,128)(2,1)} %cen.1, bf16[128,128]{1,0:T(8,128)(2,1)} %targ.1, f32[256,128]{1,0:T(8,128)} %coef.1, f32[1,256,256]{2,1,0:T(8,128)} %inv.1), custom_call_target="tpu_custom_call" | custom-call | flops 805306368 | bytes 786432 | tf_op jit(solution)/shard_map/pallas_call | solution.py:309
  32.4 0.0 copy-done
  32.4 0.0 copy-done.1
  32.4 0.0 copy-start.2
  32.4 1.7 %multiply_subtract_fusion = (f32[256,128]{1,0:T(8,128)}, f32[256,128]{1,0:T(8,128)}) fusion(f32[256,128]{1,0:T(8,128)S(1)} %copy-done, f32[256,128]{1,0:T(8,128)} %get-tuple-element.6, f32[256,128]{1,0:T(8,128)S(1)} %copy-done.1), kind=kLoop, calls=%fused_computation | loop fusion | flops 163840 | bytes 655360 | tf_op jit(solution)/shard_map/sub | solution.py:347
  34.1 0.0 copy-done.2
  34.1 0.6 %copy.10 = f32[128,128]{1,0:T(8,128)} copy(f32[128,128]{1,0:T(8,128)S(1)} %copy-done.2) | data formatting | bytes 131072
Async XLA Ops:
  0.6 31.8 %copy-start = (f32[256,128]{1,0:T(8,128)S(1)}, f32[256,128]{1,0:T(8,128)}, u32[]{:S(2)}) copy-start(f32[256,128]{1,0:T(8,128)} %coef.1) | copy-start | bytes 393220
  0.6 31.8 %copy-start.1 = (f32[256,128]{1,0:T(8,128)S(1)}, f32[256,128]{1,0:T(8,128)}, u32[]{:S(2)}) copy-start(f32[256,128]{1,0:T(8,128)} %param.10) | copy-start | bytes 393220
  32.4 1.7 %copy-start.2 = (f32[128,128]{1,0:T(8,128)S(1)}, f32[128,128]{1,0:T(8,128)}, u32[]{:S(2)}) copy-start(f32[128,128]{1,0:T(8,128)} %get-tuple-element.12) | copy-start | bytes 196612

commit v3 on v2

--- a/solution.py
+++ b/solution.py
@@ -11,8 +11,8 @@
 MESH = pl.DeviceIdType.MESH
 PRED = jnp.bfloat16
 GRAD = jnp.bfloat16
-H = 2
-Q = 4
+H = 1
+Q = 1
 
 
 def kernel(
@@ -62,10 +62,20 @@
     for load in loads:
         load.start()
 
-    def row_copy(block, d, h):
-        to = a + 1 if d == 0 else a - 1
+    def row_copy(block, d, step, h):
+        to = a + step if d == 0 else a - step
         part = rows.at[block, pl.ds(h * (R // H), R // H)]
-        return put(part, part, row_ss.at[block, d, h], row_rs.at[block, h], dev(to, b, c))
+        return put(part, part, row_ss.at[block, d, step - 1, h], row_rs.at[block, h], dev(to, b, c))
+
+    def onward(block, d, pieces, act):
+        for step in (2, 1):
+            @pl.when(a + step < A if d == 0 else a - step >= 0)
+            def _():
+                for h in pieces:
+                    act(row_copy(block, d, step, h))
+
+    start = lambda copy: copy.start()
+    wait_send = lambda copy: copy.wait_send()
 
     def cen_copy(cb, slot, q, to):
         part = cens.at[cb, pl.ds(q * (C // Q), C // Q)]
@@ -78,15 +88,8 @@
     loads[1].wait()
     pl.semaphore_wait(barrier, A - 1 + 2 * B - 1)
 
-    @pl.when(a < A - 1)
-    def _():
-        for h in range(H):
-            row_copy(a, 0, h).start()
-
-    @pl.when(a > 0)
-    def _():
-        for h in range(H):
-            row_copy(a, 1, h).start()
+    onward(a, 0, range(H), start)
+    onward(a, 1, range(H), start)
 
     for j in range(1, B):
         bb = lax.rem(b + j, B)
@@ -148,16 +151,10 @@
         def _():
             fn(a + dist, 1)
 
-    def pass_rows(h, block, d):
-        row_copy(block, d, h).wait_recv()
-        if d == 0:
-            @pl.when(a < A - 1)
-            def _():
-                row_copy(block, 0, h).start()
-        else:
-            @pl.when(a > 0)
-            def _():
-                row_copy(block, 1, h).start()
+    def pass_rows(h, dist, block, d):
+        row_copy(block, d, 1, h).wait_recv()
+        if dist % 2 == 0:
+            onward(block, d, [h], start)
 
     def near(block, d):
         row_norm(block)
@@ -177,23 +174,25 @@
     tile(a, mate_cb)
 
     steps = itertools.zip_longest(
-        [(dist, h) for dist in range(1, A - 1) for h in range(H)],
+        [(dist, h) for dist in range(2, A - 1) for h in range(H)],
         [(j, q) for j in range(1, B) for q in range(Q)],
     )
     for row_step, cen_step in steps:
         if row_step is not None:
             dist, h = row_step
-            each_at(dist, functools.partial(pass_rows, h))
+            each_at(dist, functools.partial(pass_rows, h, dist))
         if cen_step is not None:
             pass_centres(*cen_step)
-        if row_step is not None and h == H - 1:
-            each_at(dist, near)
 
     for j in range(1, B):
         bb = lax.rem(b + j, B)
         coef_copy(bb * 2 + c, 0, mate).wait_recv()
         coef_copy(bb * 2 + c, B + bb, mate).start()
         cen_norm(bb * 2 + c)
+    for h in range(H):
+        each_at(1, functools.partial(pass_rows, h, 1))
+    for dist in range(1, A - 1):
+        each_at(dist, near)
     for j in range(1, B):
         bb = lax.rem(b + j, B)
         for q in range(Q):
@@ -211,7 +210,7 @@
 
     def last(block, d):
         for h in range(H):
-            pass_rows(h, block, d)
+            pass_rows(h, A - 1, block, d)
         row_norm(block)
         tiles(block, 0, 2 * B)
         predict_and_send(block)
@@ -265,22 +264,10 @@
             inv_own[i], g_own[at, :], precision=lax.Precision.HIGHEST, preferred_element_type=jnp.float32
         )
 
-    def sent_rows(block, d):
-        if d == 0:
-            @pl.when(a < A - 1)
-            def _():
-                for h in range(H):
-                    row_copy(block, 0, h).wait_send()
-        else:
-            @pl.when(a > 0)
-            def _():
-                for h in range(H):
-                    row_copy(block, 1, h).wait_send()
-
-    sent_rows(a, 0)
-    sent_rows(a, 1)
-    for dist in range(1, A):
-        each_at(dist, sent_rows)
+    onward(a, 0, range(H), wait_send)
+    onward(a, 1, range(H), wait_send)
+    for dist in range(2, A, 2):
+        each_at(dist, lambda block, d: onward(block, d, range(H), wait_send))
     for j in range(1, B):
         bb = lax.rem(b + j, B)
         for slot in (bb, B + bb):
@@ -329,7 +316,7 @@
             pltpu.VMEM((C, K), jnp.float32),
             pltpu.VMEM((G, C, K), GRAD),
             pltpu.VMEM((G, C, K), GRAD),
-            dma((A, 2, H)), dma((A, H)),
+            dma((A, 2, 2, H)), dma((A, H)),
             dma((G, Q)), dma((G, Q)), dma((G,)), dma((G,)),
             dma((A,)), dma((A,)), dma((A,)), dma((A,)),
             dma((G,)), dma((G,)),
@@ -343,8 +330,24 @@
             transcendentals=A * R * G * C,
         ),
     )(features, centres, targets, coefficients, block_inverse)
-    new_momentum = 0.9 * momentum + conditioned / (A * B * 2 * R)
-    return residual, new_momentum, coefficients - 0.5 * new_momentum
+    return pl.pallas_call(
+        functools.partial(update, float(A * B * 2 * R)),
+        out_shape=(
+            jax.ShapeDtypeStruct((R, K), jnp.float32),
+            jax.ShapeDtypeStruct((C, K), jnp.float32),
+            jax.ShapeDtypeStruct((C, K), jnp.float32),
+        ),
+        in_specs=[vmem] * 4,
+        out_specs=(vmem,) * 3,
+
+    )(residual, conditioned, momentum, coefficients)
+
+
+def update(batch, res, cond, mom, coef, res_out, mom_out, coef_out):
+    res_out[...] = res[...]
+    new = 0.9 * mom[...] + cond[...] / batch
+    mom_out[...] = new
+    coef_out[...] = coef[...] - 0.5 * new
 
 
 def solution(mesh):

time: 34.9 us -> 33.7 us (0.966)
  other arithmetic: 1.66 us -> 0 us
  Pallas kernels: 31.7 us -> 32.9 us
  local copies, waits for them, and re-layouts: 0.64 us -> 0 us
    pallas_call x0 -> x1, Pallas kernels: none -> 1.81 us  [shards(): pl.pallas_call(functools.partial(update, float(A * B * 2 * R)), out_shape...]
    sub x1 -> x0, other arithmetic: 1.66 us -> none  [shards(): return (residual, new_momentum, coefficients - 0.5 * new_momentum)]
    unnamed x7 -> x0, local copies, waits for them, and re-layouts: 0.64 us -> none
    pallas_call x1, Pallas kernels: 31.7 us -> 31.1 us  [shards(): pl.pallas_call(functools.partial(kernel, A, B), out_shape=(jax.ShapeDtype...]
where the time goes in v3:
time: 33.7 us; the launch traced here: 33.5 us
  Pallas kernels  32.9 us (98%)
  between operations  0.64 us (2%)
    pallas_call x1, Pallas kernels, shards(): pl.pallas_call(functools.partial(kernel, A, B), out_shape=(jax.ShapeDtype...  31.1 us
    pallas_call x1, Pallas kernels, shards(): pl.pallas_call(functools.partial(update, float(A * B * 2 * R)), out_shape...  1.81 us

profile of v3, /device:TPU:1, one launch (start us, length us, event | category | flops | bytes accessed | tf_op | source)
XLA Modules:
  0.0 33.5 jit_solution(13597720371110810474)
XLA Ops:
  0.6 31.1 %shard_map.85 = (f32[128,128]{1,0:T(8,128)}, f32[256,128]{1,0:T(8,128)}) custom-call(bf16[128,512]{1,0:T(8,128)(2,1)} %feat.1, bf16[256,512]{1,0:T(8,128)(2,1)} %cen.1, bf16[128,128]{1,0:T(8,128)(2,1)} %targ.1, f32[256,128]{1,0:T(8,128)} %coef.3, f32[1,256,256]{2,1,0:T(8,128)} %inv.1), custom_call_target="tpu_custom_call" | custom-call | flops 805306368 | bytes 786432 | tf_op jit(solution)/shard_map/pallas_call | solution.py:296
  31.7 1.8 %shard_map.86 = (f32[128,128]{1,0:T(8,128)}, f32[256,128]{1,0:T(8,128)}, f32[256,128]{1,0:T(8,128)}) custom-call(f32[128,128]{1,0:T(8,128)} %get-tuple-element.5.res, f32[256,128]{1,0:T(8,128)} %get-tuple-element.6.cond, f32[256,128]{1,0:T(8,128)} %mom.1, f32[256,128]{1,0:T(8,128)} %coef.3), custom_call_target="tpu_custom_call" | custom-call | tf_op jit(solution)/shard_map/pallas_call | solution.py:333

commit v4 on v3

--- a/solution.py
+++ b/solution.py
@@ -126,14 +126,14 @@
             tile(block, lax.rem(b + i // 2, B) * 2 + lax.rem(c + lax.rem(i, 2), 2))
             return carry
 
-        lax.fori_loop(lo, hi, step, 0, unroll=2)
+        lax.fori_loop(lo, hi, step, 0, unroll=hi - lo)
 
     def predict(block):
         def step(i, acc):
             k = kt[i, :, pl.ds(pl.multiple_of(block * R, R), R)]
             return acc + jnp.dot(coefs[i], k, preferred_element_type=jnp.float32)
 
-        return lax.fori_loop(0, 2 * B, step, jnp.zeros((coefs.shape[1], R), jnp.float32), unroll=2)
+        return lax.fori_loop(0, 2 * B, step, jnp.zeros((coefs.shape[1], R), jnp.float32), unroll=4)
 
     def pred_copy(block):
         return put(pred_tx.at[block], pred_rx.at[a], pr_ss.at[block], pr_rs.at[a], dev(block, b, c))
@@ -168,11 +168,6 @@
     row_norm(a)
     cen_norm(me_cb)
     tile(a, me_cb)
-    for q in range(Q):
-        cen_copy(mate_cb, 0, q, mate).wait_recv()
-    cen_norm(mate_cb)
-    tile(a, mate_cb)
-
     steps = itertools.zip_longest(
         [(dist, h) for dist in range(2, A - 1) for h in range(H)],
         [(j, q) for j in range(1, B) for q in range(Q)],
@@ -189,6 +184,11 @@
         coef_copy(bb * 2 + c, 0, mate).wait_recv()
         coef_copy(bb * 2 + c, B + bb, mate).start()
         cen_norm(bb * 2 + c)
+    for q in range(Q):
+        cen_copy(mate_cb, 0, q, mate).wait_recv()
+    cen_norm(mate_cb)
+    tile(a, mate_cb)
+
     for h in range(H):
         each_at(1, functools.partial(pass_rows, h, 1))
     for dist in range(1, A - 1):

time: 33.7 us -> 33.4 us (level)
  no operation moved by 1% of the time
where the time goes in v4:
time: 33.4 us; the launch traced here: 33.3 us
  Pallas kernels  32.6 us (98%)
  between operations  0.64 us (2%)
    pallas_call x1, Pallas kernels, shards(): pl.pallas_call(functools.partial(kernel, A, B), out_shape=(jax.ShapeDtype...  30.8 us
    pallas_call x1, Pallas kernels, shards(): pl.pallas_call(functools.partial(update, float(A * B * 2 * R)), out_shape...  1.81 us

profile of v4, /device:TPU:1, one launch (start us, length us, event | category | flops | bytes accessed | tf_op | source)
XLA Modules:
  0.0 33.3 jit_solution(4175484405659574928)
XLA Ops:
  0.6 30.8 %shard_map.85 = (f32[128,128]{1,0:T(8,128)}, f32[256,128]{1,0:T(8,128)}) custom-call(bf16[128,512]{1,0:T(8,128)(2,1)} %feat.1, bf16[256,512]{1,0:T(8,128)(2,1)} %cen.1, bf16[128,128]{1,0:T(8,128)(2,1)} %targ.1, f32[256,128]{1,0:T(8,128)} %coef.3, f32[1,256,256]{2,1,0:T(8,128)} %inv.1), custom_call_target="tpu_custom_call" | custom-call | flops 805306368 | bytes 786432 | tf_op jit(solution)/shard_map/pallas_call | solution.py:296
  31.4 1.8 %shard_map.86 = (f32[128,128]{1,0:T(8,128)}, f32[256,128]{1,0:T(8,128)}, f32[256,128]{1,0:T(8,128)}) custom-call(f32[128,128]{1,0:T(8,128)} %get-tuple-element.5.res, f32[256,128]{1,0:T(8,128)} %get-tuple-element.6.cond, f32[256,128]{1,0:T(8,128)} %mom.1, f32[256,128]{1,0:T(8,128)} %coef.3), custom_call_target="tpu_custom_call" | custom-call | tf_op jit(solution)/shard_map/pallas_call | solution.py:333
